TPU v7x, 128 devices: a whole 4x4x4 slice. The times are simulated.
128 devices in a mesh: gz: 128 (over z, x, y, core).
Axes of the slice: x: 4, y: 4, z: 4, core: 2. Of those that a mesh axis runs over, the one named last changes fastest.
Arguments:
- features: bfloat16 [4096, 64, 512], P('gz'), may hold values from -6 to 6
- counts: int32 [128], P('gz'), may hold values from 2 to 30, as said below
- neighbors: int32 [6, 4096], P(None, 'gz'), may hold values from -1 to 4095, as said below
- weight_one: bfloat16 [27, 64, 64], replicated, may hold values from -0.15625 to 0.15625
- weight_two: bfloat16 [27, 64, 64], replicated, may hold values from -0.15625 to 0.15625
- scale_one: float32 [64], replicated, may hold values from 0.1 to 1.9
- shift_one: float32 [64], replicated, may hold values from -3 to 3
- scale_two: float32 [64], replicated, may hold values from 0.1 to 1.9
- shift_two: float32 [64], replicated, may hold values from -3 to 3
Outputs:
- bricks_out: bfloat16 [4096, 64, 512], P('gz')
Inputs may be any that keep to these rules, and one draw needn't show every extreme that they name: `counts`: device i and device i + 64 hold together at most 32 live bricks, and some such pair holds exactly 32. A device's live bricks are its slots below its count. Only live bricks have and are neighbors. Symmetric: if neighbors[k, g] = h then neighbors[k xor 1, h] = g. Two different devices share at most one face. Device i shares a face with devices i + d and i - d modulo 128 for d = 1 to 5, and with device i + 128 / 2 modulo 128, and with no others.
All inputs are finite; a program needn't handle non-finite values.
Results may differ from a plain program's by a relative error of at most 0.0038.
Values may be sent and summed in bfloat16 or wider, within the bound.
A program may use at most 128 MiB of HBM per device.

v0:
```python
import jax
import jax.numpy as jnp
from jax import lax
from jax.experimental import pallas as pl
from jax.experimental.pallas import tpu as pltpu
from jax.sharding import PartitionSpec as P

C = 64
BR = 8
CAP = 32
HALF = CAP // 2
VOX = BR**3
LANES = CAP * BR
PARK = 30 * BR
ROWS = 3 * C
OFFSETS = (1, 2, 3, 4, 5, -1, -2, -3, -4, -5, 64)
PEERS = len(OFFSETS)
INVERSE = tuple(OFFSETS.index(-o) if abs(o) < 64 else PEERS - 1 for o in OFFSETS)
F32 = jnp.float32
BF16 = jnp.bfloat16


def dot(a, b):
    return jnp.dot(a, b, preferred_element_type=F32)


def dot_nt(a, b):
    return lax.dot_general(a, b, (((1,), (1,)), ((), ())), preferred_element_type=F32)


def iota(shape, dim):
    return lax.broadcasted_iota(jnp.int32, shape, dim)


def one_hot(condition):
    return jnp.where(condition, 1.0, 0.0).astype(BF16)


def column(row):
    wide = jnp.broadcast_to(row, (C, C))
    return jnp.sum(jnp.where(iota((C, C), 0) == iota((C, C), 1), wide, 0.0), axis=1, keepdims=True)


def center(x, y):
    return x + 1, pl.ds(ROWS * (y + 1) + C, C)


def kernel(
    feat_hbm, counts_ref, nbr_hbm, w1_hbm, w2_hbm, s1_hbm, t1_hbm, s2_hbm, t2_hbm,
    act_hbm,
    feat, nbv, w_raw, rows, z1, z2, wa, wb, affine, regroup, act,
    g_near, g_far, g_send, g_shift, g_inner, send_buf, recv_buf, unpack, remote,
    load_sem, send_sem, recv_sem, save_sem,
):
    devices = lax.axis_size("gz")
    me = lax.axis_index("gz")
    loads = [
        pltpu.make_async_copy(feat_hbm, feat, load_sem.at[0]),
        pltpu.make_async_copy(nbr_hbm, nbv, load_sem.at[1]),
        pltpu.make_async_copy(w1_hbm, w_raw.at[0], load_sem.at[2]),
        pltpu.make_async_copy(w2_hbm, w_raw.at[1], load_sem.at[3]),
    ]
    for i, ref in enumerate((s1_hbm, t1_hbm, s2_hbm, t2_hbm)):
        loads.append(pltpu.make_async_copy(ref, rows.at[i], load_sem.at[4 + i]))
    for load in loads:
        load.start()
    peers = [lax.rem(me + (o + devices), devices) for o in OFFSETS]
    barrier = pltpu.get_barrier_semaphore()
    for peer in peers:
        pl.semaphore_signal(
            barrier, inc=1, device_id=(peer,), device_id_type=pl.DeviceIdType.MESH
        )

    corner = jnp.zeros((ROWS, LANES), BF16)
    for z in (z1, z2):
        for x in (0, BR + 1):
            for y in (0, BR + 1):
                z[x, ROWS * y : ROWS * y + ROWS, :] = corner
    recv_buf[:, PEERS:] = jnp.zeros((2, 16 - PEERS, 16, 256), BF16)

    loads[1].wait()
    table = jnp.concatenate([nbv[...], jnp.full((2, CAP), -1, jnp.int32)], axis=0)
    dist = ((table >> 5) - me + 2 * devices) & (devices - 1)
    peer_at = jnp.where(dist == 64, PEERS - 1, jnp.where(dist <= 5, dist - 1, 132 - dist))
    code = jnp.where(dist == 0, table & (CAP - 1), CAP + peer_at)
    code = jnp.where(table < 0, -1, code).astype(F32).astype(BF16)
    widen = one_hot(iota((CAP, LANES), 0) == iota((CAP, LANES), 1) >> 3)
    wide = dot(code, widen).astype(jnp.int32) * 8
    lane_z = iota((1, LANES), 1) & 7
    wide = [jnp.where(wide[k : k + 1] < 0, -4096, wide[k : k + 1]) for k in range(6)]
    peer = [(wide[k] >> 3) - CAP for k in range(6)]
    lane = iota((1, LANES), 1)
    row_near = iota((LANES, LANES), 0)
    row_far = iota((128, LANES), 0)
    low_edge, high_edge = lane_z == 0, lane_z == 7
    for k in range(4):
        g_near[k] = one_hot(row_near == jnp.where(peer[k] < 0, wide[k] + lane_z, -1))
        g_far[k] = one_hot(row_far == jnp.where(peer[k] < 0, -1, 16 * lane_z + peer[k]))
        g_send[k] = one_hot(row_far == jnp.where(peer[k] < 0, -1, 8 * peer[k] + lane_z))
    below = jnp.where(peer[4] < 0, wide[4] + 7, PARK + peer[4])
    above = jnp.where(peer[5] < 0, wide[5], PARK + peer[5])
    g_shift[:, 0:LANES] = one_hot(row_near == jnp.where(low_edge, below, lane - 1))
    g_shift[:, LANES:] = one_hot(row_near == jnp.where(high_edge, above, lane + 1))
    inner = one_hot(row_near == jnp.where(low_edge, -1, lane - 1))
    g_inner[:, 0:LANES] = inner
    g_inner[:, LANES:] = one_hot(row_near == jnp.where(high_edge, -1, lane + 1))
    for y in range(BR):
        key = jnp.where(high_edge, peer[5], jnp.where(low_edge, peer[4], -1))
        g_send[4 + y] = one_hot(row_far == jnp.where(key < 0, -1, 8 * key + y))

    for load in loads[2:]:
        load.wait()
    for n in range(2):
        for dy in range(3):
            pieces = [w_raw[n, 9 * (t // 3) + 3 * dy + t % 3] for t in range(8)]
            wa[n, dy * C : dy * C + C, :] = jnp.concatenate(pieces, axis=1)
        wb[n] = jnp.concatenate([w_raw[n, 20 + 3 * dy] for dy in range(3)], axis=1)
    for i in range(4):
        affine[i] = jnp.broadcast_to(column(rows[i : i + 1, :]), (C, LANES))
    loads[0].wait()

    def enter(j, carry):
        cols = pl.ds(pl.multiple_of(128 * j, 128), 128)
        for p in range(HALF):
            both = jnp.concatenate([feat[p, :, cols], feat[p + HALF, :, cols]], axis=0)
            regroup[:, p] = both.T.astype(F32).reshape(HALF, 8, 128)
        for n in range(16):
            both = regroup[n].reshape(128, 128).astype(BF16).T
            x, at = center(2 * j + n // 8, n % 8)
            z1[x, at, 0:128] = both[0:C]
            z1[x, at, 128:256] = both[C:]
        return carry

    lax.fori_loop(0, 4, enter, 0)
    pl.semaphore_wait(barrier, PEERS)

    def layer_x(z, x):
        return jnp.concatenate([z[center(x, y)] for y in range(BR)], axis=0)

    def layer_y(z, y):
        return jnp.concatenate([z[center(x, y)] for x in range(BR)], axis=0)

    def exchange(z, phase):
        picked = jnp.zeros((8 * C, 128), F32)
        faces = [layer_x(z, 0), layer_x(z, 7), layer_y(z, 0), layer_y(z, 7)]
        for k in range(4):
            picked = picked + dot_nt(faces[k], g_send[k])
        for y in range(BR):
            picked = picked + dot_nt(layer_y(z, y), g_send[4 + y])
        picked = picked.astype(BF16)
        blocks = [
            picked[128 * i : 128 * i + 128].T.astype(F32).reshape(16, 8, 128) for i in range(4)
        ]
        for i in range(2):
            pair = jnp.concatenate([blocks[2 * i], blocks[2 * i + 1]], axis=1).astype(BF16)
            send_buf[phase, :, :, 128 * i : 128 * i + 128] = pair
        copies = []
        for p in range(PEERS):
            copy = pltpu.make_async_remote_copy(
                src_ref=send_buf.at[phase, p],
                dst_ref=recv_buf.at[phase, INVERSE[p]],
                send_sem=send_sem.at[phase, p],
                recv_sem=recv_sem.at[phase, INVERSE[p]],
                device_id=(peers[p],),
                device_id_type=pl.DeviceIdType.MESH,
            )
            copy.start()
            copies.append(copy)
        for copy in copies:
            copy.wait()
        for i in range(2):
            pair = recv_buf[phase, :, :, 128 * i : 128 * i + 128].astype(F32)
            for h in range(2):
                unpack[2 * i + h] = pair[:, 8 * h : 8 * h + 8].reshape(128, 128)
        parked = iota((16, 128), 1) >= PARK - 128
        parked = jnp.concatenate([one_hot(parked)] * 8, axis=0) > 0
        for i in range(4):
            block = jnp.concatenate(
                [unpack[i, pl.ds(q, 16, stride=8), :] for q in range(BR)], axis=0
            )
            block = block.astype(BF16).T
            remote[128 * i : 128 * i + 128, :] = block
            for q in range(BR):
                shifted = pltpu.roll(block, PARK - 128 - 16 * q, 1) if q < 7 else block
                both = jnp.concatenate([z[center(2 * i + n, q)][:, 128:] for n in range(2)], axis=0)
                both = jnp.where(parked, shifted, both)
                for n in range(2):
                    x, at = center(2 * i + n, q)
                    z[x, at, 128:] = both[C * n : C * n + C]

    def fill(z):
        for k in range(4):
            face = layer_x(z, 7 - 7 * k) if k < 2 else layer_y(z, 7 - 7 * (k - 2))
            halo = dot(face, g_near[k]) + dot(remote[...], g_far[k])
            halo = halo.astype(BF16)
            sides = dot(halo, g_inner[...]).astype(BF16)
            for a in range(BR):
                if k < 2:
                    x, base = (BR + 1) * k, ROWS * (a + 1)
                else:
                    x, base = a + 1, ROWS * (BR + 1) * (k - 2)
                rows = slice(C * a, C * a + C)
                z[x, base : base + C, :] = sides[rows, 0:LANES]
                z[x, base + C : base + 2 * C, :] = halo[rows]
                z[x, base + 2 * C : base + 3 * C, :] = sides[rows, LANES:]

        def edges(y, carry):
            sides = dot(layer_y(z, y), g_shift[...]).astype(BF16)
            base = ROWS * (y + 1)
            for x in range(BR):
                z[x + 1, pl.ds(base, C), :] = sides[C * x : C * x + C, 0:LANES]
                z[x + 1, pl.ds(base + 2 * C, C), :] = sides[C * x : C * x + C, LANES:]
            return carry

        lax.fori_loop(0, BR, edges, 0)

    alive = (iota((C, LANES), 1) >> 3) < counts_ref[0]

    def convolve(z, n, store, done):
        def body(x, carry):
            products = []
            for y in range(BR + 2):
                at = slice(ROWS * y, ROWS * y + ROWS)
                stack = jnp.concatenate(
                    [z[x, at, :], z[x + 1, at, :], z[x + 2, ROWS * y : ROWS * y + 2 * C, :]], axis=0
                )
                if y == 0:
                    lhs = wa[n, 0:C]
                elif y == BR + 1:
                    lhs = wa[n, 2 * C :]
                else:
                    lhs = wa[n]
                products.append(dot(lhs, stack))
            for y in range(BR):
                last = jnp.concatenate(
                    [z[x + 2, ROWS * (y + d) + 2 * C : ROWS * (y + d) + 3 * C, :] for d in range(3)],
                    axis=0,
                )
                total = products[y][0:C] + products[y + 1][C : 2 * C]
                top = products[y + 2]
                total = total + (top if y == BR - 1 else top[2 * C :])
                total = total + dot(wb[n], last)
                store(x, y, total * affine[2 * n] + affine[2 * n + 1])
            done(x)
            return carry

        lax.fori_loop(0, BR, body, 0)

    def store_hidden(x, y, value):
        value = jnp.where(alive, jnp.maximum(value, 0.0), 0.0)
        z2[center(x, y)] = value.astype(BF16)

    def store_out(x, y, value):
        value = jnp.maximum(value + z1[center(x, y)].astype(F32), 0.0)
        act[x, y] = jnp.where(alive, value, 0.0).astype(BF16)

    def saving(x):
        return pltpu.make_async_copy(act.at[x], act_hbm.at[x], save_sem.at[x])

    exchange(z1, 0)
    fill(z1)
    convolve(z1, 0, store_hidden, lambda x: None)
    exchange(z2, 1)
    fill(z2)
    convolve(z2, 1, store_out, lambda x: saving(x).start())

    for x in range(BR):
        saving(x).wait()


def leave(act_ref, out_ref, spread):
    for n in range(16):
        value = act_ref[n // 8, n % 8]
        both = jnp.concatenate([value[:, 0:128], value[:, 128:256]], axis=0).T
        spread[:, n] = both.astype(F32).reshape(HALF, 8, 128)
    for p in range(HALF):
        both = spread[p].reshape(128, 128).astype(BF16).T
        out_ref[p] = both[0:C]
        out_ref[p + HALF] = both[C:]


def on_device(
    features, counts, neighbors, weight_one, weight_two, scale_one, shift_one, scale_two, shift_two
):
    hbm = pl.BlockSpec(memory_space=pltpu.HBM)
    smem = pl.BlockSpec(memory_space=pltpu.SMEM)
    act = pl.pallas_call(
        kernel,
        out_shape=jax.ShapeDtypeStruct((BR, BR, C, LANES), BF16),
        in_specs=[hbm, smem] + [hbm] * 7,
        out_specs=hbm,
        scratch_shapes=[
            pltpu.VMEM((CAP, C, VOX), BF16),
            pltpu.VMEM((6, CAP), jnp.int32),
            pltpu.VMEM((2, 27, C, C), BF16),
            pltpu.VMEM((4, C), F32),
            pltpu.VMEM((BR + 2, ROWS * (BR + 2), LANES), BF16),
            pltpu.VMEM((BR + 2, ROWS * (BR + 2), LANES), BF16),
            pltpu.VMEM((2, 3 * C, 8 * C), BF16),
            pltpu.VMEM((2, C, 3 * C), BF16),
            pltpu.VMEM((4, C, LANES), F32),
            pltpu.VMEM((16, HALF, 8, 128), F32),
            pltpu.VMEM((BR, BR, C, LANES), BF16),
            pltpu.VMEM((4, LANES, LANES), BF16),
            pltpu.VMEM((4, 128, LANES), BF16),
            pltpu.VMEM((12, 128, LANES), BF16),
            pltpu.VMEM((LANES, 2 * LANES), BF16),
            pltpu.VMEM((LANES, 2 * LANES), BF16),
            pltpu.VMEM((2, 16, 16, 256), BF16),
            pltpu.VMEM((2, 16, 16, 256), BF16),
            pltpu.VMEM((4, 128, 128), F32),
            pltpu.VMEM((8 * C, 128), BF16),
            pltpu.SemaphoreType.DMA((8,)),
            pltpu.SemaphoreType.DMA((2, PEERS)),
            pltpu.SemaphoreType.DMA((2, PEERS)),
            pltpu.SemaphoreType.DMA((BR,)),
        ],
        compiler_params=pltpu.CompilerParams(
            collective_id=0, has_side_effects=True, vmem_limit_bytes=61 << 20
        ),
    )(
        features, counts, neighbors, weight_one, weight_two,
        scale_one, shift_one, scale_two, shift_two,
    )
    return pl.pallas_call(
        leave,
        grid=(4,),
        out_shape=jax.ShapeDtypeStruct((CAP, C, VOX), BF16),
        in_specs=[pl.BlockSpec((2, BR, C, LANES), lambda j: (j, 0, 0, 0))],
        out_specs=pl.BlockSpec((CAP, C, 128), lambda j: (0, 0, j)),
        scratch_shapes=[pltpu.VMEM((HALF, 16, 8, 128), F32)],
        compiler_params=pltpu.CompilerParams(vmem_limit_bytes=60 << 20),
    )(act)


def solution(mesh):
    in_specs = (P("gz", None, None), P("gz"), P(None, "gz"), P(), P(), P(), P(), P(), P())
    out_specs = P("gz", None, None)
    return jax.shard_map(
        on_device, mesh=mesh, in_specs=in_specs, out_specs=out_specs, check_vma=False
    )
```

profile of v0, /device:TPU:1, one launch (start us, length us, event | category | flops | bytes accessed | tf_op | source)
XLA Modules:
  0.0 54.3 jit_solution(2005747316918346389)
XLA Ops:
  0.7 49.3 %shard_map.91.act_ref = bf16[8,8,64,256]{3,2,1,0:T(8,128)(2,1)} custom-call(bf16[32,64,512]{2,1,0:T(8,128)(2,1)} %feat_hbm.1, s32[1]{0:T(128)S(6)} %copy.10.counts_ref, s32[6,32]{1,0:T(8,128)} %nbr_hbm.1, bf16[27,64,64]{2,1,0:T(8,128)(2,1)} %w1_hbm.1, bf16[27,64,64]{2,1,0:T(8,128)(2,1)} %w2_hbm.1, f32[64]{0:T(128)} %s1_hbm.1, f32[64]{0:T(128)} %t1_hbm.1, ...), custom_call_target="tpu_custom_call" | custom-call | tf_op jit(solution)/shard_map/pallas_call | solution.py:287
  49.9 4.4 %shard_map.92 = bf16[32,64,512]{2,1,0:T(8,128)(2,1)} custom-call(bf16[8,8,64,256]{3,2,1,0:T(8,128)(2,1)} %shard_map.91.act_ref), custom_call_target="tpu_custom_call" | custom-call | tf_op jit(solution)/shard_map/pallas_call | solution.py:325
where the time goes:
time: 54.5 us; the launch traced here: 54.3 us
  Pallas kernels  53.7 us (99%)
  between operations  0.66 us (1%)
    pallas_call x1, Pallas kernels, on_device(): pl.pallas_call(kernel, out_shape=jax.ShapeDtypeStruct((BR, BR, C, LANES),...  49.3 us
    pallas_call x1, Pallas kernels, on_device(): pl.pallas_call(leave, grid=(4,), out_shape=jax.ShapeDtypeStruct((CAP, C,...  4.41 us

commit v1 on v0

v1 whole, which is shorter than its diff:
```python
import jax
import jax.numpy as jnp
from jax import lax
from jax.experimental import pallas as pl
from jax.experimental.pallas import tpu as pltpu
from jax.sharding import PartitionSpec as P

C = 64
BR = 8
CAP = 32
HALF = CAP // 2
VOX = BR**3
LANES = CAP * BR
PARKED_SLOT = 30
PARK = PARKED_SLOT * BR
ROWS = 3 * C
OFFSETS = (1, 2, 3, 4, 5, -1, -2, -3, -4, -5, 64)
PEERS = len(OFFSETS)
INVERSE = tuple(OFFSETS.index(-o) if abs(o) < 64 else PEERS - 1 for o in OFFSETS)
F32 = jnp.float32
BF16 = jnp.bfloat16


def dot(a, b):
    return jnp.dot(a, b, preferred_element_type=F32)


def dot_nt(a, b):
    return lax.dot_general(a, b, (((1,), (1,)), ((), ())), preferred_element_type=F32)


def iota(shape, dim):
    return lax.broadcasted_iota(jnp.int32, shape, dim)


def one_hot(condition):
    return jnp.where(condition, 1.0, 0.0).astype(BF16)


def column(row):
    wide = jnp.broadcast_to(row, (C, C))
    return jnp.sum(jnp.where(iota((C, C), 0) == iota((C, C), 1), wide, 0.0), axis=1, keepdims=True)


def center(x, y):
    return x + 1, pl.ds(ROWS * (y + 1) + C, C)


def kernel(
    feat_hbm, counts_ref, nbr_hbm, w1_hbm, w2_hbm, s1_hbm, t1_hbm, s2_hbm, t2_hbm,
    act_hbm, order_ref,
    feat, nbv, w_raw, rows, z1, z2, wa, wb, affine, alive, regroup, act,
    g_near, g_far, g_send, g_shift, g_inner, send_buf, recv_buf, unpack, remote,
    load_sem, send_sem, recv_sem, save_sem,
):
    devices = lax.axis_size("gz")
    me = lax.axis_index("gz")
    loads = [
        pltpu.make_async_copy(feat_hbm, feat, load_sem.at[0]),
        pltpu.make_async_copy(nbr_hbm, nbv, load_sem.at[1]),
        pltpu.make_async_copy(w1_hbm, w_raw.at[0], load_sem.at[2]),
        pltpu.make_async_copy(w2_hbm, w_raw.at[1], load_sem.at[3]),
    ]
    for i, ref in enumerate((s1_hbm, t1_hbm, s2_hbm, t2_hbm)):
        loads.append(pltpu.make_async_copy(ref, rows.at[i], load_sem.at[4 + i]))
    for load in loads:
        load.start()
    peers = [lax.rem(me + (o + devices), devices) for o in OFFSETS]
    barrier = pltpu.get_barrier_semaphore()
    for peer in peers:
        pl.semaphore_signal(
            barrier, inc=1, device_id=(peer,), device_id_type=pl.DeviceIdType.MESH
        )

    corner = jnp.zeros((ROWS, 128), BF16)
    for z in (z1, z2):
        for g in range(2):
            for x in (0, BR + 1):
                for y in (0, BR + 1):
                    z[g, x, ROWS * y : ROWS * y + ROWS, :] = corner
    recv_buf[:, PEERS:] = jnp.zeros((2, 16 - PEERS, 16, 256), BF16)

    loads[1].wait()
    table = nbv[...]
    dist = ((table >> 5) - me + 2 * devices) & (devices - 1)
    peer_at = jnp.where(dist == 64, PEERS - 1, jnp.where(dist <= 5, dist - 1, 132 - dist))
    borders = jnp.where((table >= 0) & (dist != 0), 1.0, 0.0)
    borders = jnp.max(borders, axis=0, keepdims=True)
    slot = iota((1, CAP), 1)
    usable = slot < PARKED_SLOT
    flags = jnp.concatenate(
        [jnp.where(usable, borders, 0.0), jnp.where(usable, 1.0 - borders, 0.0)]
        + [jnp.zeros((6, CAP), F32)], axis=0,
    ).astype(BF16)
    ranks = dot(flags, one_hot(iota((CAP, CAP), 0) < iota((CAP, CAP), 1)))
    plain = jnp.sum(flags[1:2].astype(F32), axis=1, keepdims=True)
    place = jnp.where(borders > 0.5, plain + ranks[0:1], ranks[1:2])
    place = jnp.where(usable, place.astype(jnp.int32), slot)
    square = iota((CAP, CAP), 0) == iota((CAP, CAP), 1)
    place_column = jnp.sum(
        jnp.where(square, jnp.broadcast_to(place, (CAP, CAP)), 0), axis=1, keepdims=True
    )
    order = [jnp.sum(jnp.where(place == s, slot, 0)) for s in range(CAP)]
    order = [jnp.clip(s, 0, CAP - 1) for s in order]
    for s in range(CAP):
        order_ref[s] = order[s]

    codes = []
    for k in range(6):
        local = jnp.where(iota((CAP, CAP), 0) == (table[k : k + 1] & (CAP - 1)), place_column, 0)
        local = jnp.sum(local, axis=0, keepdims=True)
        code = jnp.where(dist[k : k + 1] == 0, local, CAP + peer_at[k : k + 1])
        codes.append(jnp.where(table[k : k + 1] < 0, -1, code))
    codes.append((slot < counts_ref[0]).astype(jnp.int32))
    codes.append(jnp.zeros((1, CAP), jnp.int32))
    codes = jnp.concatenate(codes, axis=0).astype(F32).astype(BF16)
    wide = dot(codes, one_hot(place_column == iota((CAP, LANES), 1) >> 3)).astype(jnp.int32)
    alive_row = wide[6:7]
    wide = [jnp.where(wide[k : k + 1] < 0, -4096, wide[k : k + 1] * 8) for k in range(6)]
    peer = [(wide[k] >> 3) - CAP for k in range(6)]
    lane = iota((1, LANES), 1)
    lane_z = lane & 7
    row_near = iota((LANES, LANES), 0)
    row_far = iota((128, 128), 0)
    low_edge, high_edge = lane_z == 0, lane_z == 7
    for k in range(4):
        g_near[k] = one_hot(row_near == jnp.where(peer[k] < 0, wide[k] + lane_z, -1))
        far = peer[k][:, 128:]
        z_far = lane_z[:, 128:]
        g_far[k] = one_hot(row_far == jnp.where(far < 0, -1, 16 * z_far + far))
        g_send[k] = one_hot(row_far == jnp.where(far < 0, -1, 8 * far + z_far))
    below = jnp.where(peer[4] < 0, wide[4] + 7, PARK + peer[4])
    above = jnp.where(peer[5] < 0, wide[5], PARK + peer[5])
    before = one_hot(row_near == jnp.where(low_edge, below, lane - 1))
    after = one_hot(row_near == jnp.where(high_edge, above, lane + 1))
    for g in range(2):
        cols = slice(128 * g, 128 * g + 128)
        g_shift[g] = jnp.concatenate([before[:, cols], after[:, cols]], axis=1)
    lane, edge = lane[:, 0:128], lane_z[:, 0:128]
    g_inner[:, 0:128] = one_hot(row_far == jnp.where(edge == 0, -1, lane - 1))
    g_inner[:, 128:] = one_hot(row_far == jnp.where(edge == 7, -1, lane + 1))
    for y in range(BR):
        key = jnp.where(high_edge, peer[5], jnp.where(low_edge, peer[4], -1))[:, 128:]
        g_send[4 + y] = one_hot(row_far == jnp.where(key < 0, -1, 8 * key + y))
    for i in range(2):
        alive[i] = jnp.broadcast_to(alive_row[:, 128 * i : 128 * i + 128], (8, 128)).astype(F32)

    for load in loads[2:]:
        load.wait()
    for n in range(2):
        for dy in range(3):
            pieces = [w_raw[n, 9 * (t // 3) + 3 * dy + t % 3] for t in range(8)]
            wa[n, dy * C : dy * C + C, :] = jnp.concatenate(pieces, axis=1)
        wb[n] = jnp.concatenate([w_raw[n, 20 + 3 * dy] for dy in range(3)], axis=1)
    for i in range(4):
        affine[i] = jnp.broadcast_to(column(rows[i : i + 1, :]), (C, 128))
    loads[0].wait()

    def enter(j, carry):
        cols = pl.ds(pl.multiple_of(128 * j, 128), 128)
        for p in range(HALF):
            both = jnp.concatenate([feat[order[p], :, cols], feat[order[p + HALF], :, cols]], axis=0)
            regroup[:, p] = both.T.astype(F32).reshape(HALF, 8, 128)
        for n in range(16):
            both = regroup[n].reshape(128, 128).astype(BF16).T
            x, at = center(2 * j + n // 8, n % 8)
            z1[0, x, at, :] = both[0:C]
            z1[1, x, at, :] = both[C:]
        return carry

    lax.fori_loop(0, 4, enter, 0)

    def block(z, g, x, y):
        return z[(g,) + center(x, y)]

    def both_groups(z, x, y):
        return jnp.concatenate([block(z, 0, x, y), block(z, 1, x, y)], axis=1)

    def layer(read, x=None, y=None):
        at = [(x, i) if y is None else (i, y) for i in range(BR)]
        return jnp.concatenate([read(*i) for i in at], axis=0)

    def send(z, phase):
        def read(x, y):
            return block(z, 1, x, y)

        faces = [layer(read, x=0), layer(read, x=7), layer(read, y=0), layer(read, y=7)]
        faces += [layer(read, y=y) for y in range(BR)]
        picked = jnp.zeros((8 * C, 128), F32)
        for k in range(12):
            picked = picked + dot_nt(faces[k], g_send[k])
        picked = picked.astype(BF16)
        blocks = [
            picked[128 * i : 128 * i + 128].T.astype(F32).reshape(16, 8, 128) for i in range(4)
        ]
        for i in range(2):
            pair = jnp.concatenate([blocks[2 * i], blocks[2 * i + 1]], axis=1).astype(BF16)
            send_buf[phase, :, :, 128 * i : 128 * i + 128] = pair
        if phase == 0:
            pl.semaphore_wait(barrier, PEERS)
        copies = []
        for p in range(PEERS):
            copy = pltpu.make_async_remote_copy(
                src_ref=send_buf.at[phase, p],
                dst_ref=recv_buf.at[phase, INVERSE[p]],
                send_sem=send_sem.at[phase, p],
                recv_sem=recv_sem.at[phase, INVERSE[p]],
                device_id=(peers[p],),
                device_id_type=pl.DeviceIdType.MESH,
            )
            copy.start()
            copies.append(copy)
        return copies

    def receive(z, phase, copies):
        for copy in copies:
            copy.wait()
        for i in range(2):
            pair = recv_buf[phase, :, :, 128 * i : 128 * i + 128].astype(F32)
            for h in range(2):
                unpack[2 * i + h] = pair[:, 8 * h : 8 * h + 8].reshape(128, 128)
        parked = one_hot(iota((16, 128), 1) >= PARK - 128)
        parked = jnp.concatenate([parked] * 8, axis=0) > 0
        for i in range(4):
            got = jnp.concatenate(
                [unpack[i, pl.ds(q, 16, stride=8), :] for q in range(BR)], axis=0
            )
            got = got.astype(BF16).T
            remote[128 * i : 128 * i + 128, :] = got
            for q in range(BR):
                shifted = pltpu.roll(got, PARK - 128 - 16 * q, 1) if q < 7 else got
                both = jnp.concatenate([block(z, 1, 2 * i + n, q) for n in range(2)], axis=0)
                both = jnp.where(parked, shifted, both)
                for n in range(2):
                    z[(1,) + center(2 * i + n, q)] = both[C * n : C * n + C]

    def fill(z, g):
        def read(x, y):
            return both_groups(z, x, y)

        cols = slice(128 * g, 128 * g + 128)
        for k in range(4):
            face = layer(read, x=7 - 7 * k) if k < 2 else layer(read, y=7 - 7 * (k - 2))
            halo = dot(face, g_near[k, :, cols])
            if g == 1:
                halo = halo + dot(remote[...], g_far[k])
            halo = halo.astype(BF16)
            sides = dot(halo, g_inner[...]).astype(BF16)
            for a in range(BR):
                if k < 2:
                    x, base = (BR + 1) * k, ROWS * (a + 1)
                else:
                    x, base = a + 1, ROWS * (BR + 1) * (k - 2)
                rows = slice(C * a, C * a + C)
                z[g, x, base : base + C, :] = sides[rows, 0:128]
                z[g, x, base + C : base + 2 * C, :] = halo[rows]
                z[g, x, base + 2 * C : base + 3 * C, :] = sides[rows, 128:]

        def edges(y, carry):
            sides = dot(layer(read, y=y), g_shift[g]).astype(BF16)
            base = ROWS * (y + 1)
            for x in range(BR):
                z[g, x + 1, pl.ds(base, C), :] = sides[C * x : C * x + C, 0:128]
                z[g, x + 1, pl.ds(base + 2 * C, C), :] = sides[C * x : C * x + C, 128:]
            return carry

        lax.fori_loop(0, BR, edges, 0)

    def convolve(z, n, g, store, done):
        live = jnp.concatenate([alive[g]] * 8, axis=0) > 0.5

        def body(i, carry):
            pair = [2 * i, 2 * i + 1]
            products = []
            for y in range(BR + 2):
                at = slice(ROWS * y, ROWS * y + ROWS)
                stack = jnp.concatenate(
                    [
                        jnp.concatenate(
                            [z[g, x, at, :], z[g, x + 1, at, :]]
                            + [z[g, x + 2, ROWS * y : ROWS * y + 2 * C, :]], axis=0,
                        )
                        for x in pair
                    ], axis=1,
                )
                if y == 0:
                    lhs = wa[n, 0:C]
                elif y == BR + 1:
                    lhs = wa[n, 2 * C :]
                else:
                    lhs = wa[n]
                products.append(dot(lhs, stack))
            for y in range(BR):
                last = jnp.concatenate(
                    [
                        jnp.concatenate(
                            [
                                z[g, x + 2, ROWS * (y + d) + 2 * C : ROWS * (y + d) + 3 * C, :]
                                for d in range(3)
                            ], axis=0,
                        )
                        for x in pair
                    ], axis=1,
                )
                total = products[y][0:C] + products[y + 1][C : 2 * C]
                top = products[y + 2]
                total = total + (top if y == BR - 1 else top[2 * C :])
                total = total + dot(wb[n], last)
                for m, x in enumerate(pair):
                    value = total[:, 128 * m : 128 * m + 128] * affine[2 * n] + affine[2 * n + 1]
                    store(g, x, y, value, live)
            for x in pair:
                done(g, x)
            return carry

        lax.fori_loop(0, BR // 2, body, 0)

    def store_hidden(g, x, y, value, live):
        value = jnp.where(live, jnp.maximum(value, 0.0), 0.0)
        z2[(g,) + center(x, y)] = value.astype(BF16)

    def store_out(g, x, y, value, live):
        value = jnp.maximum(value + block(z1, g, x, y).astype(F32), 0.0)
        act[g, x, y] = jnp.where(live, value, 0.0).astype(BF16)

    def saving(g, x):
        return pltpu.make_async_copy(act.at[g, x], act_hbm.at[g, x], save_sem.at[g, x])

    def nothing(g, x):
        pass

    def save(g, x):
        saving(g, x).start()

    copies = send(z1, 0)
    fill(z1, 0)
    convolve(z1, 0, 0, store_hidden, nothing)
    receive(z1, 0, copies)
    fill(z1, 1)
    convolve(z1, 0, 1, store_hidden, nothing)
    copies = send(z2, 1)
    fill(z2, 0)
    convolve(z2, 1, 0, store_out, save)
    receive(z2, 1, copies)
    fill(z2, 1)
    convolve(z2, 1, 1, store_out, save)
    for g in range(2):
        for x in range(BR):
            saving(g, x).wait()


def leave(order_ref, act_ref, out_ref, spread):
    for n in range(16):
        both = act_ref[:, n // 8, n % 8].reshape(128, 128).T
        spread[:, n] = both.astype(F32).reshape(HALF, 8, 128)
    for p in range(HALF):
        both = spread[p].reshape(128, 128).astype(BF16).T
        out_ref[order_ref[p]] = both[0:C]
        out_ref[order_ref[p + HALF]] = both[C:]


def on_device(
    features, counts, neighbors, weight_one, weight_two, scale_one, shift_one, scale_two, shift_two
):
    hbm = pl.BlockSpec(memory_space=pltpu.HBM)
    smem = pl.BlockSpec(memory_space=pltpu.SMEM)
    act, order = pl.pallas_call(
        kernel,
        out_shape=(
            jax.ShapeDtypeStruct((2, BR, BR, C, 128), BF16),
            jax.ShapeDtypeStruct((CAP,), jnp.int32),
        ),
        in_specs=[hbm, smem] + [hbm] * 7,
        out_specs=(hbm, smem),
        scratch_shapes=[
            pltpu.VMEM((CAP, C, VOX), BF16),
            pltpu.VMEM((6, CAP), jnp.int32),
            pltpu.VMEM((2, 27, C, C), BF16),
            pltpu.VMEM((4, C), F32),
            pltpu.VMEM((2, BR + 2, ROWS * (BR + 2), 128), BF16),
            pltpu.VMEM((2, BR + 2, ROWS * (BR + 2), 128), BF16),
            pltpu.VMEM((2, 3 * C, 8 * C), BF16),
            pltpu.VMEM((2, C, 3 * C), BF16),
            pltpu.VMEM((4, C, 128), F32),
            pltpu.VMEM((2, 8, 128), F32),
            pltpu.VMEM((16, HALF, 8, 128), F32),
            pltpu.VMEM((2, BR, BR, C, 128), BF16),
            pltpu.VMEM((4, LANES, LANES), BF16),
            pltpu.VMEM((4, 128, 128), BF16),
            pltpu.VMEM((12, 128, 128), BF16),
            pltpu.VMEM((2, LANES, LANES), BF16),
            pltpu.VMEM((128, 256), BF16),
            pltpu.VMEM((2, 16, 16, 256), BF16),
            pltpu.VMEM((2, 16, 16, 256), BF16),
            pltpu.VMEM((4, 128, 128), F32),
            pltpu.VMEM((8 * C, 128), BF16),
            pltpu.SemaphoreType.DMA((8,)),
            pltpu.SemaphoreType.DMA((2, PEERS)),
            pltpu.SemaphoreType.DMA((2, PEERS)),
            pltpu.SemaphoreType.DMA((2, BR)),
        ],
        compiler_params=pltpu.CompilerParams(
            collective_id=0, has_side_effects=True, vmem_limit_bytes=61 << 20
        ),
    )(
        features, counts, neighbors, weight_one, weight_two,
        scale_one, shift_one, scale_two, shift_two,
    )
    return pl.pallas_call(
        leave,
        grid=(4,),
        out_shape=jax.ShapeDtypeStruct((CAP, C, VOX), BF16),
        in_specs=[smem, pl.BlockSpec((2, 2, BR, C, 128), lambda j: (0, j, 0, 0, 0))],
        out_specs=pl.BlockSpec((CAP, C, 128), lambda j: (0, 0, j)),
        scratch_shapes=[pltpu.VMEM((HALF, 16, 8, 128), F32)],
        compiler_params=pltpu.CompilerParams(vmem_limit_bytes=60 << 20),
    )(order, act)


def solution(mesh):
    in_specs = (P("gz", None, None), P("gz"), P(None, "gz"), P(), P(), P(), P(), P(), P())
    out_specs = P("gz", None, None)
    return jax.shard_map(
        on_device, mesh=mesh, in_specs=in_specs, out_specs=out_specs, check_vma=False
    )
```

time: 54.5 us -> 43.7 us (0.80)
  Pallas kernels: 53.7 us -> 42.8 us
    pallas_call x1, Pallas kernels: 49.3 us -> 38.4 us  [on_device(): pl.pallas_call(kernel, out_shape=(jax.ShapeDtypeStruct((2, BR, BR, C, 128...]
where the time goes in v1:
time: 43.7 us; the launch traced here: 43.5 us
  Pallas kernels  42.8 us (98%)
  between operations  0.66 us (2%)
    pallas_call x1, Pallas kernels, on_device(): pl.pallas_call(kernel, out_shape=(jax.ShapeDtypeStruct((2, BR, BR, C, 128...  38.4 us
    pallas_call x1, Pallas kernels, on_device(): pl.pallas_call(leave, grid=(4,), out_shape=jax.ShapeDtypeStruct((CAP, C,...  4.44 us

profile of v1, /device:TPU:1, one launch (start us, length us, event | category | flops | bytes accessed | tf_op | source)
XLA Modules:
  0.0 43.5 jit_solution(14305372763721364421)
XLA Ops:
  0.7 38.4 %shard_map.91 = (bf16[2,8,8,64,128]{4,3,2,1,0:T(8,128)(2,1)}, s32[32]{0:T(128)}) custom-call(bf16[32,64,512]{2,1,0:T(8,128)(2,1)} %feat_hbm.1, s32[1]{0:T(128)S(6)} %copy.10.counts_ref, s32[6,32]{1,0:T(8,128)} %nbr_hbm.1, bf16[27,64,64]{2,1,0:T(8,128)(2,1)} %w1_hbm.1, bf16[27,64,64]{2,1,0:T(8,128)(2,1)} %w2_hbm.1, f32[64]{0:T(128)} %s1_hbm.1, f32[64]{0:T(128)} %t1_hbm.1, ...), custom_call_target="tpu_custom_call" | custom-call | tf_op jit(solution)/shard_map/pallas_call | solution.py:367
  39.0 4.4 %shard_map.92 = bf16[32,64,512]{2,1,0:T(8,128)(2,1)} custom-call(s32[32]{0:T(128)} %get-tuple-element.7.order_ref, bf16[2,8,8,64,128]{4,3,2,1,0:T(8,128)(2,1)} %get-tuple-element.8.act_ref), custom_call_target="tpu_custom_call" | custom-call | tf_op jit(solution)/shard_map/pallas_call | solution.py:409

commit v2 on v1

--- a/solution.py
+++ b/solution.py
@@ -48,10 +48,10 @@
 
 def kernel(
     feat_hbm, counts_ref, nbr_hbm, w1_hbm, w2_hbm, s1_hbm, t1_hbm, s2_hbm, t2_hbm,
-    act_hbm, order_ref,
-    feat, nbv, w_raw, rows, z1, z2, wa, wb, affine, alive, regroup, act,
+    spread_ref, order_ref,
+    feat, nbv, w_raw, rows, z1, z2, wa, wb, affine, alive, regroup, act, turned,
     g_near, g_far, g_send, g_shift, g_inner, send_buf, recv_buf, unpack, remote,
-    load_sem, send_sem, recv_sem, save_sem,
+    load_sem, send_sem, recv_sem,
 ):
     devices = lax.axis_size("gz")
     me = lax.axis_index("gz")
@@ -264,7 +264,8 @@
                 z[g, x + 1, pl.ds(base + 2 * C, C), :] = sides[C * x : C * x + C, 128:]
             return carry
 
-        lax.fori_loop(0, BR, edges, 0)
+        for y in range(BR):
+            edges(y, 0)
 
     def convolve(z, n, g, store, done):
         live = jnp.concatenate([alive[g]] * 8, axis=0) > 0.5
@@ -313,7 +314,8 @@
                 done(g, x)
             return carry
 
-        lax.fori_loop(0, BR // 2, body, 0)
+        for i in range(BR // 2):
+            body(i, 0)
 
     def store_hidden(g, x, y, value, live):
         value = jnp.where(live, jnp.maximum(value, 0.0), 0.0)
@@ -321,16 +323,21 @@
 
     def store_out(g, x, y, value, live):
         value = jnp.maximum(value + block(z1, g, x, y).astype(F32), 0.0)
-        act[g, x, y] = jnp.where(live, value, 0.0).astype(BF16)
-
-    def saving(g, x):
-        return pltpu.make_async_copy(act.at[g, x], act_hbm.at[g, x], save_sem.at[g, x])
+        value = jnp.where(live, value, 0.0).astype(BF16)
+        if g == 0:
+            act[x, y] = value
+        else:
+            both = jnp.concatenate([act[x, y], value], axis=0).T
+            turned[x, y] = both.astype(F32).reshape(HALF, 8, 128)
 
     def nothing(g, x):
         pass
 
-    def save(g, x):
-        saving(g, x).start()
+    def spread(g, x):
+        for y in range(0, BR, 2):
+            pair = jnp.concatenate([turned[x, y], turned[x, y + 1]], axis=1).astype(BF16)
+            at = 64 * x + 8 * y
+            spread_ref[:, at : at + 16, :] = pair
 
     copies = send(z1, 0)
     fill(z1, 0)
@@ -340,23 +347,25 @@
     convolve(z1, 0, 1, store_hidden, nothing)
     copies = send(z2, 1)
     fill(z2, 0)
-    convolve(z2, 1, 0, store_out, save)
+    convolve(z2, 1, 0, store_out, nothing)
     receive(z2, 1, copies)
     fill(z2, 1)
-    convolve(z2, 1, 1, store_out, save)
-    for g in range(2):
-        for x in range(BR):
-            saving(g, x).wait()
-
-
-def leave(order_ref, act_ref, out_ref, spread):
-    for n in range(16):
-        both = act_ref[:, n // 8, n % 8].reshape(128, 128).T
-        spread[:, n] = both.astype(F32).reshape(HALF, 8, 128)
+    convolve(z2, 1, 1, store_out, spread)
+
+
+def leave(order_ref, spread_ref, out_hbm, bricks, save_sem):
+    saves = []
     for p in range(HALF):
-        both = spread[p].reshape(128, 128).astype(BF16).T
-        out_ref[order_ref[p]] = both[0:C]
-        out_ref[order_ref[p + HALF]] = both[C:]
+        for j in range(4):
+            both = spread_ref[p, 128 * j : 128 * j + 128, :].T
+            bricks[p, :, 128 * j : 128 * j + 128] = both[0:C]
+            bricks[p + HALF, :, 128 * j : 128 * j + 128] = both[C:]
+        for s in (p, p + HALF):
+            save = pltpu.make_async_copy(bricks.at[s], out_hbm.at[order_ref[s]], save_sem.at[s])
+            save.start()
+            saves.append(save)
+    for save in saves:
+        save.wait()
 
 
 def on_device(
@@ -364,14 +373,18 @@
 ):
     hbm = pl.BlockSpec(memory_space=pltpu.HBM)
     smem = pl.BlockSpec(memory_space=pltpu.SMEM)
-    act, order = pl.pallas_call(
+    vmem = pl.BlockSpec(memory_space=pltpu.VMEM)
+    arrays = [features, neighbors, weight_one, weight_two]
+    arrays += [scale_one, shift_one, scale_two, shift_two]
+    features, *rest = [pltpu.with_memory_space_constraint(a, pltpu.HBM) for a in arrays]
+    spread, order = pl.pallas_call(
         kernel,
         out_shape=(
-            jax.ShapeDtypeStruct((2, BR, BR, C, 128), BF16),
+            pltpu.VMEM((HALF, VOX, 128), BF16),
             jax.ShapeDtypeStruct((CAP,), jnp.int32),
         ),
         in_specs=[hbm, smem] + [hbm] * 7,
-        out_specs=(hbm, smem),
+        out_specs=(vmem, smem),
         scratch_shapes=[
             pltpu.VMEM((CAP, C, VOX), BF16),
             pltpu.VMEM((6, CAP), jnp.int32),
@@ -384,7 +397,8 @@
             pltpu.VMEM((4, C, 128), F32),
             pltpu.VMEM((2, 8, 128), F32),
             pltpu.VMEM((16, HALF, 8, 128), F32),
-            pltpu.VMEM((2, BR, BR, C, 128), BF16),
+            pltpu.VMEM((BR, BR, C, 128), BF16),
+            pltpu.VMEM((BR, BR, HALF, 8, 128), F32),
             pltpu.VMEM((4, LANES, LANES), BF16),
             pltpu.VMEM((4, 128, 128), BF16),
             pltpu.VMEM((12, 128, 128), BF16),
@@ -397,24 +411,21 @@
             pltpu.SemaphoreType.DMA((8,)),
             pltpu.SemaphoreType.DMA((2, PEERS)),
             pltpu.SemaphoreType.DMA((2, PEERS)),
-            pltpu.SemaphoreType.DMA((2, BR)),
         ],
         compiler_params=pltpu.CompilerParams(
-            collective_id=0, has_side_effects=True, vmem_limit_bytes=61 << 20
+            collective_id=0, has_side_effects=True, vmem_limit_bytes=48 << 20
         ),
     )(
-        features, counts, neighbors, weight_one, weight_two,
-        scale_one, shift_one, scale_two, shift_two,
+        features, counts, *rest
     )
     return pl.pallas_call(
         leave,
-        grid=(4,),
         out_shape=jax.ShapeDtypeStruct((CAP, C, VOX), BF16),
-        in_specs=[smem, pl.BlockSpec((2, 2, BR, C, 128), lambda j: (0, j, 0, 0, 0))],
-        out_specs=pl.BlockSpec((CAP, C, 128), lambda j: (0, 0, j)),
-        scratch_shapes=[pltpu.VMEM((HALF, 16, 8, 128), F32)],
-        compiler_params=pltpu.CompilerParams(vmem_limit_bytes=60 << 20),
-    )(order, act)
+        in_specs=[smem, vmem],
+        out_specs=hbm,
+        scratch_shapes=[pltpu.VMEM((CAP, C, VOX), BF16), pltpu.SemaphoreType.DMA((CAP,))],
+        compiler_params=pltpu.CompilerParams(vmem_limit_bytes=8 << 20),
+    )(order, spread)
 
 
 def solution(mesh):

time: 43.7 us -> 34.7 us (0.79)
  Pallas kernels: 42.8 us -> 33.7 us
    pallas_call x2, Pallas kernels: 42.8 us -> 33.7 us  [the longest x1 31.5 us: on_device(): pl.pallas_call(kernel, out_shape=(pltpu.VMEM((HALF, VOX, 128), BF16), jax...]
where the time goes in v2:
time: 34.7 us; the launch traced here: 34.5 us
  Pallas kernels  33.7 us (97%)
  between operations  0.82 us (2%)
    pallas_call x1, Pallas kernels, on_device(): pl.pallas_call(kernel, out_shape=(pltpu.VMEM((HALF, VOX, 128), BF16), jax...  31.5 us
    pallas_call x1, Pallas kernels, on_device(): pl.pallas_call(leave, out_shape=jax.ShapeDtypeStruct((CAP, C, VOX), BF16)...  2.2 us

profile of v2, /device:TPU:1, one launch (start us, length us, event | category | flops | bytes accessed | tf_op | source)
XLA Modules:
  0.0 34.5 jit_solution(14867598003771763048)
XLA Ops:
  0.7 31.5 %shard_map.91 = (bf16[16,512,128]{2,1,0:T(8,128)(2,1)S(1)}, s32[32]{0:T(128)S(1)}) custom-call(bf16[32,64,512]{2,1,0:T(8,128)(2,1)} %feat_hbm.1, s32[1]{0:T(128)S(6)} %copy.10.counts_ref, s32[6,32]{1,0:T(8,128)} %nbr_hbm.1, bf16[27,64,64]{2,1,0:T(8,128)(2,1)} %w1_hbm.1, bf16[27,64,64]{2,1,0:T(8,128)(2,1)} %w2_hbm.1, f32[64]{0:T(128)} %s1_hbm.1, f32[64]{0:T(128)} %t1_hbm.1, ...), custom_call_target="tpu_custom_call" | custom-call | tf_op jit(solution)/shard_map/pallas_call | solution.py:380
  32.2 2.2 %shard_map.92 = bf16[32,64,512]{2,1,0:T(8,128)(2,1)} custom-call(s32[32]{0:T(128)S(1)} %get-tuple-element.7.order_ref, bf16[16,512,128]{2,1,0:T(8,128)(2,1)S(1)} %get-tuple-element.8.spread_ref), custom_call_target="tpu_custom_call" | custom-call | tf_op jit(solution)/shard_map/pallas_call | solution.py:421

commit v3 on v2

--- a/solution.py
+++ b/solution.py
@@ -50,7 +50,7 @@
     feat_hbm, counts_ref, nbr_hbm, w1_hbm, w2_hbm, s1_hbm, t1_hbm, s2_hbm, t2_hbm,
     spread_ref, order_ref,
     feat, nbv, w_raw, rows, z1, z2, wa, wb, affine, alive, regroup, act, turned,
-    g_near, g_far, g_send, g_shift, g_inner, send_buf, recv_buf, unpack, remote,
+    g_near, g_far, g_send, g_shift, send_buf, recv_buf, unpack, remote,
     load_sem, send_sem, recv_sem,
 ):
     devices = lax.axis_size("gz")
@@ -72,15 +72,17 @@
             barrier, inc=1, device_id=(peer,), device_id_type=pl.DeviceIdType.MESH
         )
 
-    corner = jnp.zeros((ROWS, 128), BF16)
-    for z in (z1, z2):
-        for g in range(2):
-            for x in (0, BR + 1):
-                for y in (0, BR + 1):
-                    z[g, x, ROWS * y : ROWS * y + ROWS, :] = corner
     recv_buf[:, PEERS:] = jnp.zeros((2, 16 - PEERS, 16, 256), BF16)
 
-    loads[1].wait()
+    for load in loads:
+        load.wait()
+    for n in range(2):
+        for dy in range(3):
+            pieces = [w_raw[n, 9 * (t // 3) + 3 * dy + t % 3] for t in range(8)]
+            wa[n, dy * C : dy * C + C, :] = jnp.concatenate(pieces, axis=1)
+        wb[n] = jnp.concatenate([w_raw[n, 20 + 3 * dy] for dy in range(3)], axis=1)
+    for i in range(4):
+        affine[i] = jnp.broadcast_to(column(rows[i : i + 1, :]), (C, 128))
     table = nbv[...]
     dist = ((table >> 5) - me + 2 * devices) & (devices - 1)
     peer_at = jnp.where(dist == 64, PEERS - 1, jnp.where(dist <= 5, dist - 1, 132 - dist))
@@ -120,44 +122,20 @@
     peer = [(wide[k] >> 3) - CAP for k in range(6)]
     lane = iota((1, LANES), 1)
     lane_z = lane & 7
-    row_near = iota((LANES, LANES), 0)
     row_far = iota((128, 128), 0)
     low_edge, high_edge = lane_z == 0, lane_z == 7
     for k in range(4):
-        g_near[k] = one_hot(row_near == jnp.where(peer[k] < 0, wide[k] + lane_z, -1))
         far = peer[k][:, 128:]
-        z_far = lane_z[:, 128:]
-        g_far[k] = one_hot(row_far == jnp.where(far < 0, -1, 16 * z_far + far))
-        g_send[k] = one_hot(row_far == jnp.where(far < 0, -1, 8 * far + z_far))
-    below = jnp.where(peer[4] < 0, wide[4] + 7, PARK + peer[4])
-    above = jnp.where(peer[5] < 0, wide[5], PARK + peer[5])
-    before = one_hot(row_near == jnp.where(low_edge, below, lane - 1))
-    after = one_hot(row_near == jnp.where(high_edge, above, lane + 1))
-    for g in range(2):
-        cols = slice(128 * g, 128 * g + 128)
-        g_shift[g] = jnp.concatenate([before[:, cols], after[:, cols]], axis=1)
-    lane, edge = lane[:, 0:128], lane_z[:, 0:128]
-    g_inner[:, 0:128] = one_hot(row_far == jnp.where(edge == 0, -1, lane - 1))
-    g_inner[:, 128:] = one_hot(row_far == jnp.where(edge == 7, -1, lane + 1))
+        half = slice(128 * (k % 2), 128 * (k % 2) + 128)
+        key = jnp.where(far < 0, -1, 8 * far + lane_z[:, 128:])
+        g_send[k // 2, :, half] = one_hot(row_far == key)
     for y in range(BR):
         key = jnp.where(high_edge, peer[5], jnp.where(low_edge, peer[4], -1))[:, 128:]
-        g_send[4 + y] = one_hot(row_far == jnp.where(key < 0, -1, 8 * key + y))
-    for i in range(2):
-        alive[i] = jnp.broadcast_to(alive_row[:, 128 * i : 128 * i + 128], (8, 128)).astype(F32)
-
-    for load in loads[2:]:
-        load.wait()
-    for n in range(2):
-        for dy in range(3):
-            pieces = [w_raw[n, 9 * (t // 3) + 3 * dy + t % 3] for t in range(8)]
-            wa[n, dy * C : dy * C + C, :] = jnp.concatenate(pieces, axis=1)
-        wb[n] = jnp.concatenate([w_raw[n, 20 + 3 * dy] for dy in range(3)], axis=1)
-    for i in range(4):
-        affine[i] = jnp.broadcast_to(column(rows[i : i + 1, :]), (C, 128))
-    loads[0].wait()
+        half = slice(128 * (y % 2), 128 * (y % 2) + 128)
+        g_send[2 + y // 2, :, half] = one_hot(row_far == jnp.where(key < 0, -1, 8 * key + y))
 
     def enter(j, carry):
-        cols = pl.ds(pl.multiple_of(128 * j, 128), 128)
+        cols = slice(128 * j, 128 * j + 128)
         for p in range(HALF):
             both = jnp.concatenate([feat[order[p], :, cols], feat[order[p + HALF], :, cols]], axis=0)
             regroup[:, p] = both.T.astype(F32).reshape(HALF, 8, 128)
@@ -168,7 +146,8 @@
             z1[1, x, at, :] = both[C:]
         return carry
 
-    lax.fori_loop(0, 4, enter, 0)
+    for j in range(4):
+        enter(j, 0)
 
     def block(z, g, x, y):
         return z[(g,) + center(x, y)]
@@ -187,8 +166,9 @@
         faces = [layer(read, x=0), layer(read, x=7), layer(read, y=0), layer(read, y=7)]
         faces += [layer(read, y=y) for y in range(BR)]
         picked = jnp.zeros((8 * C, 128), F32)
-        for k in range(12):
-            picked = picked + dot_nt(faces[k], g_send[k])
+        for k in range(6):
+            pair = jnp.concatenate(faces[2 * k : 2 * k + 2], axis=1)
+            picked = picked + dot_nt(pair, g_send[k])
         picked = picked.astype(BF16)
         blocks = [
             picked[128 * i : 128 * i + 128].T.astype(F32).reshape(16, 8, 128) for i in range(4)
@@ -234,27 +214,41 @@
                 for n in range(2):
                     z[(1,) + center(2 * i + n, q)] = both[C * n : C * n + C]
 
+    low_lanes = one_hot((iota((16, 128), 1) & 7) == 0)
+    high_lanes = one_hot((iota((16, 128), 1) & 7) == 7)
+
     def fill(z, g):
         def read(x, y):
             return both_groups(z, x, y)
 
-        cols = slice(128 * g, 128 * g + 128)
-        for k in range(4):
-            face = layer(read, x=7 - 7 * k) if k < 2 else layer(read, y=7 - 7 * (k - 2))
-            halo = dot(face, g_near[k, :, cols])
-            if g == 1:
-                halo = halo + dot(remote[...], g_far[k])
-            halo = halo.astype(BF16)
-            sides = dot(halo, g_inner[...]).astype(BF16)
-            for a in range(BR):
-                if k < 2:
-                    x, base = (BR + 1) * k, ROWS * (a + 1)
-                else:
-                    x, base = a + 1, ROWS * (BR + 1) * (k - 2)
-                rows = slice(C * a, C * a + C)
-                z[g, x, base : base + C, :] = sides[rows, 0:128]
-                z[g, x, base + C : base + 2 * C, :] = halo[rows]
-                z[g, x, base + 2 * C : base + 3 * C, :] = sides[rows, 128:]
+        def planes(k, a):
+            if k < 2:
+                return (BR + 1) * k, ROWS * (a + 1)
+            return a + 1, ROWS * (BR + 1) * (k - 2)
+
+        def put(x, base, value):
+            low = jnp.concatenate([low_lanes] * (C // 16), axis=0) > 0
+            high = jnp.concatenate([high_lanes] * (C // 16), axis=0) > 0
+            zero = jnp.zeros((C, 128), BF16)
+            z[g, x, base : base + C, :] = jnp.where(low, zero, pltpu.roll(value, 1, 1))
+            z[g, x, base + C : base + 2 * C, :] = value
+            z[g, x, base + 2 * C : base + 3 * C, :] = jnp.where(high, zero, pltpu.roll(value, 127, 1))
+
+        if g == 0:
+            for k in range(4):
+                face = layer(read, x=7 - 7 * k) if k < 2 else layer(read, y=7 - 7 * (k - 2))
+                halo = dot(face, g_near[k]).astype(BF16)
+                for a in range(BR):
+                    x, base = planes(k, a)
+                    put(x, base, halo[C * a : C * a + C, 0:128])
+                    z[1, x, base + C : base + 2 * C, :] = halo[C * a : C * a + C, 128:]
+        else:
+            far = dot(remote[...], g_far[...]).astype(BF16)
+            for k in range(4):
+                for a in range(BR):
+                    x, base = planes(k, a)
+                    local = z[1, x, base + C : base + 2 * C, :]
+                    put(x, base, local + far[C * a : C * a + C, 128 * k : 128 * k + 128])
 
         def edges(y, carry):
             sides = dot(layer(read, y=y), g_shift[g]).astype(BF16)
@@ -339,6 +333,28 @@
             at = 64 * x + 8 * y
             spread_ref[:, at : at + 16, :] = pair
 
+    row_near = iota((LANES, LANES), 0)
+    for k in range(4):
+        g_near[k] = one_hot(row_near == jnp.where(peer[k] < 0, wide[k] + lane_z, -1))
+        far = peer[k][:, 128:]
+        key = jnp.where(far < 0, -1, 16 * lane_z[:, 128:] + far)
+        g_far[:, 128 * k : 128 * k + 128] = one_hot(row_far == key)
+    below = jnp.where(peer[4] < 0, wide[4] + 7, PARK + peer[4])
+    above = jnp.where(peer[5] < 0, wide[5], PARK + peer[5])
+    before = one_hot(row_near == jnp.where(low_edge, below, lane - 1))
+    after = one_hot(row_near == jnp.where(high_edge, above, lane + 1))
+    for g in range(2):
+        cols = slice(128 * g, 128 * g + 128)
+        g_shift[g] = jnp.concatenate([before[:, cols], after[:, cols]], axis=1)
+    for i in range(2):
+        alive[i] = jnp.broadcast_to(alive_row[:, 128 * i : 128 * i + 128], (8, 128)).astype(F32)
+
+    corner = jnp.zeros((ROWS, 128), BF16)
+    for z in (z1, z2):
+        for g in range(2):
+            for x in (0, BR + 1):
+                for y in (0, BR + 1):
+                    z[g, x, ROWS * y : ROWS * y + ROWS, :] = corner
     copies = send(z1, 0)
     fill(z1, 0)
     convolve(z1, 0, 0, store_hidden, nothing)
@@ -400,10 +416,9 @@
             pltpu.VMEM((BR, BR, C, 128), BF16),
             pltpu.VMEM((BR, BR, HALF, 8, 128), F32),
             pltpu.VMEM((4, LANES, LANES), BF16),
-            pltpu.VMEM((4, 128, 128), BF16),
-            pltpu.VMEM((12, 128, 128), BF16),
+            pltpu.VMEM((128, 512), BF16),
+            pltpu.VMEM((6, 128, 256), BF16),
             pltpu.VMEM((2, LANES, LANES), BF16),
-            pltpu.VMEM((128, 256), BF16),
             pltpu.VMEM((2, 16, 16, 256), BF16),
             pltpu.VMEM((2, 16, 16, 256), BF16),
             pltpu.VMEM((4, 128, 128), F32),

time: 34.7 us -> 33.3 us (0.960)
  Pallas kernels: 33.7 us -> 32.4 us
    pallas_call x1, Pallas kernels: 31.5 us -> 30.2 us  [on_device(): pl.pallas_call(kernel, out_shape=(pltpu.VMEM((HALF, VOX, 128), BF16), jax...]
where the time goes in v3:
time: 33.3 us; the launch traced here: 33.2 us
  Pallas kernels  32.4 us (97%)
  between operations  0.82 us (2%)
    pallas_call x1, Pallas kernels, on_device(): pl.pallas_call(kernel, out_shape=(pltpu.VMEM((HALF, VOX, 128), BF16), jax...  30.2 us
    pallas_call x1, Pallas kernels, on_device(): pl.pallas_call(leave, out_shape=jax.ShapeDtypeStruct((CAP, C, VOX), BF16)...  2.2 us

profile of v3, /device:TPU:1, one launch (start us, length us, event | category | flops | bytes accessed | tf_op | source)
XLA Modules:
  0.0 33.2 jit_solution(10226547421871801498)
XLA Ops:
  0.7 30.2 %shard_map.91 = (bf16[16,512,128]{2,1,0:T(8,128)(2,1)S(1)}, s32[32]{0:T(128)S(1)}) custom-call(bf16[32,64,512]{2,1,0:T(8,128)(2,1)} %feat_hbm.1, s32[1]{0:T(128)S(6)} %copy.10.counts_ref, s32[6,32]{1,0:T(8,128)} %nbr_hbm.1, bf16[27,64,64]{2,1,0:T(8,128)(2,1)} %w1_hbm.1, bf16[27,64,64]{2,1,0:T(8,128)(2,1)} %w2_hbm.1, f32[64]{0:T(128)} %s1_hbm.1, f32[64]{0:T(128)} %t1_hbm.1, ...), custom_call_target="tpu_custom_call" | custom-call | tf_op jit(solution)/shard_map/pallas_call | solution.py:396
  30.8 2.2 %shard_map.92 = bf16[32,64,512]{2,1,0:T(8,128)(2,1)} custom-call(s32[32]{0:T(128)S(1)} %get-tuple-element.7.order_ref, bf16[16,512,128]{2,1,0:T(8,128)(2,1)S(1)} %get-tuple-element.8.spread_ref), custom_call_target="tpu_custom_call" | custom-call | tf_op jit(solution)/shard_map/pallas_call | solution.py:436

commit v4 on v3

--- a/solution.py
+++ b/solution.py
@@ -17,6 +17,7 @@
 OFFSETS = (1, 2, 3, 4, 5, -1, -2, -3, -4, -5, 64)
 PEERS = len(OFFSETS)
 INVERSE = tuple(OFFSETS.index(-o) if abs(o) < 64 else PEERS - 1 for o in OFFSETS)
+FAR_FIRST = sorted(range(PEERS), key=lambda p: -abs(OFFSETS[p]))
 F32 = jnp.float32
 BF16 = jnp.bfloat16
 
@@ -179,7 +180,7 @@
         if phase == 0:
             pl.semaphore_wait(barrier, PEERS)
         copies = []
-        for p in range(PEERS):
+        for p in FAR_FIRST:
             copy = pltpu.make_async_remote_copy(
                 src_ref=send_buf.at[phase, p],
                 dst_ref=recv_buf.at[phase, INVERSE[p]],

time: 33.3 us -> 33.2 us (level)
  no operation moved by 1% of the time
where the time goes in v4:
time: 33.2 us; the launch traced here: 33.1 us
  Pallas kernels  32.2 us (97%)
  between operations  0.82 us (2%)
    pallas_call x1, Pallas kernels, on_device(): pl.pallas_call(kernel, out_shape=(pltpu.VMEM((HALF, VOX, 128), BF16), jax...  30.1 us
    pallas_call x1, Pallas kernels, on_device(): pl.pallas_call(leave, out_shape=jax.ShapeDtypeStruct((CAP, C, VOX), BF16)...  2.2 us

profile of v4, /device:TPU:1, one launch (start us, length us, event | category | flops | bytes accessed | tf_op | source)
XLA Modules:
  0.0 33.1 jit_solution(4486749378529638143)
XLA Ops:
  0.7 30.1 %shard_map.91 = (bf16[16,512,128]{2,1,0:T(8,128)(2,1)S(1)}, s32[32]{0:T(128)S(1)}) custom-call(bf16[32,64,512]{2,1,0:T(8,128)(2,1)} %feat_hbm.1, s32[1]{0:T(128)S(6)} %copy.10.counts_ref, s32[6,32]{1,0:T(8,128)} %nbr_hbm.1, bf16[27,64,64]{2,1,0:T(8,128)(2,1)} %w1_hbm.1, bf16[27,64,64]{2,1,0:T(8,128)(2,1)} %w2_hbm.1, f32[64]{0:T(128)} %s1_hbm.1, f32[64]{0:T(128)} %t1_hbm.1, ...), custom_call_target="tpu_custom_call" | custom-call | tf_op jit(solution)/shard_map/pallas_call | solution.py:397
  30.7 2.2 %shard_map.92 = bf16[32,64,512]{2,1,0:T(8,128)(2,1)} custom-call(s32[32]{0:T(128)S(1)} %get-tuple-element.7.order_ref, bf16[16,512,128]{2,1,0:T(8,128)(2,1)S(1)} %get-tuple-element.8.spread_ref), custom_call_target="tpu_custom_call" | custom-call | tf_op jit(solution)/shard_map/pallas_call | solution.py:437
